TPU v7x, 32 devices: a whole 2x2x4 slice. The times are simulated.
32 devices in a mesh: seq: 8 (over z, x), head: 4 (over y, core).
Axes of the slice: x: 2, y: 2, z: 4, core: 2. Of those that a mesh axis runs over, the one named last changes fastest.
Arguments:
- queries: bfloat16 [2048, 2048], P('seq', 'head'), may hold values from -180 to 180
- keys: bfloat16 [2048, 2048], P('seq', 'head'), may hold values from -7 to 7
- values: bfloat16 [2048, 2048], P('seq', 'head'), may hold values from -6 to 6
- out_grad: bfloat16 [2048, 2048], P('seq', 'head'), may hold values from -6 to 6
- rand_blocks: int32 [32, 3], replicated, may hold values from 0 to 31, as said below
- glob_blocks: int32 [8], P('seq'), may hold values from 0 to 31, as said below
Outputs:
- attn_out: bfloat16 [2048, 2048], P('seq', 'head')
- query_grad: bfloat16 [2048, 2048], P('seq', 'head')
- key_grad: bfloat16 [2048, 2048], P('seq', 'head')
- value_grad: bfloat16 [2048, 2048], P('seq', 'head')
Inputs may be any that keep to these rules, and one draw needn't show every extreme that they name: `rand_blocks`: rows 4 * i to 4 * (i + 1) - 1 are the query blocks of index i of seq. Among their 12 entries, the blocks of any one index j of seq (blocks 4 * j to 4 * (j + 1) - 1) are named at most 2 times; in every draw one index j is named exactly 2 times by the rows of every index i. `glob_blocks`: entry j is one of the blocks 4 * j to 4 * (j + 1) - 1.
All inputs are finite; a program needn't handle non-finite values.
Results may differ from a plain program's by a relative error of at most 0.0052.
Values may be sent and summed in bfloat16 or wider, within the bound.
A program may use at most 128 MiB of HBM per device.

v0:
```python
import math
import jax
import jax.numpy as jnp
from jax import lax
from jax.sharding import PartitionSpec as P

HDIM = 128
BLK = 64
GLEN = 16


def extended(array, sides, width):
    for axis, dim in sides:
        size, length = (lax.axis_size(axis), array.shape[dim])
        up = [(i, (i + 1) % size) for i in range(size - 1)]
        down = [(j, i) for i, j in up]
        last = lax.slice_in_dim(array, length - width, length, axis=dim)
        first = lax.slice_in_dim(array, 0, width, axis=dim)
        before = lax.ppermute(last, axis, up)
        after = lax.ppermute(first, axis, down)
        array = jnp.concatenate([before, array, after], axis=dim)
    return array


def shards(queries, keys, values, out_grad, rand_blocks, glob_blocks):
    rows_dev, width_dev = queries.shape
    head_count = width_dev // HDIM
    seq_count = lax.axis_size("seq")
    my_index = lax.axis_index("seq")
    blocks_dev = rows_dev // BLK
    total_blocks = blocks_dev * seq_count
    per_block = rand_blocks.shape[1]
    spots = blocks_dev * per_block
    capacity = max(2, (spots + seq_count - 1) // seq_count)
    scale = 1.0 / math.sqrt(HDIM)
    local_len = (3 + per_block) * BLK
    global_len = seq_count * GLEN
    paired = jnp.stack([keys, values], 1)
    padded = extended(paired, (("seq", 0),), BLK)
    earlier = padded[:rows_dev].reshape(blocks_dev, BLK, 2, width_dev)
    current = paired.reshape(blocks_dev, BLK, 2, width_dev)
    later = padded[2 * BLK :].reshape(blocks_dev, BLK, 2, width_dev)
    own_global = glob_blocks[0] - my_index * blocks_dev
    mine = lax.dynamic_slice_in_dim(paired, own_global * BLK, GLEN, 0)
    global_kv = lax.all_gather(mine, "seq", axis=0, tiled=True)
    plan = rand_blocks.reshape(seq_count, spots)
    owners = plan // blocks_dev
    targets = plan % blocks_dev
    member = (owners[:, :, None] == jnp.arange(seq_count, dtype=jnp.int32)[None, None, :]).astype(
        jnp.int32
    )
    ranks = jnp.sum(member * (jnp.cumsum(member, axis=1) - 1), axis=2)
    places = owners * capacity + ranks
    my_places = lax.dynamic_index_in_dim(places, my_index, 0, keepdims=False)
    asked = (
        (owners == my_index)[:, :, None]
        & (ranks[:, :, None] == jnp.arange(capacity, dtype=jnp.int32)[None, None, :])
    ).astype(jnp.int32)
    incoming = jnp.sum(asked * (targets[:, :, None] + 1), axis=1) - 1
    block_kv = paired.reshape(blocks_dev, BLK, 2, width_dev)
    outgoing = jnp.take(block_kv, jnp.maximum(incoming, 0), axis=0)
    received = lax.all_to_all(outgoing, "seq", split_axis=0, concat_axis=0, tiled=True)
    fetched = jnp.take(received.reshape(seq_count * capacity, BLK, 2, width_dev), my_places, axis=0)
    fetched = fetched.reshape(blocks_dev, per_block * BLK, 2, width_dev)
    local_kv = jnp.concatenate([earlier, current, later, fetched], 1)
    query_blocks = queries.reshape(blocks_dev, BLK, head_count, HDIM)
    grad_blocks = out_grad.reshape(blocks_dev, BLK, head_count, HDIM)
    local_keys = local_kv[:, :, 0].reshape(blocks_dev, local_len, head_count, HDIM)
    local_vals = local_kv[:, :, 1].reshape(blocks_dev, local_len, head_count, HDIM)
    global_keys = global_kv[:, 0].reshape(global_len, head_count, HDIM)
    global_vals = global_kv[:, 1].reshape(global_len, head_count, HDIM)
    block_ids = my_index * blocks_dev + jnp.arange(blocks_dev, dtype=jnp.int32)
    before_ok = jnp.broadcast_to((block_ids > 0)[:, None], (blocks_dev, BLK))
    after_ok = jnp.broadcast_to((block_ids < total_blocks - 1)[:, None], (blocks_dev, BLK))
    visible = jnp.concatenate(
        [
            before_ok,
            jnp.ones((blocks_dev, BLK), bool),
            after_ok,
            jnp.ones((blocks_dev, per_block * BLK), bool),
        ],
        1,
    )
    scores_local = (
        jnp.einsum("bqhd,bkhd->bhqk", query_blocks, local_keys, preferred_element_type=jnp.float32)
        * scale
    )
    scores_local = jnp.where(visible[:, None, None, :], scores_local, -jnp.inf)
    scores_global = (
        jnp.einsum("bqhd,khd->bhqk", query_blocks, global_keys, preferred_element_type=jnp.float32)
        * scale
    )
    top = jnp.maximum(
        jnp.max(scores_local, axis=-1, keepdims=True),
        jnp.max(scores_global, axis=-1, keepdims=True),
    )
    expo_local = jnp.exp(scores_local - top)
    expo_global = jnp.exp(scores_global - top)
    totals = jnp.sum(expo_local, axis=-1, keepdims=True) + jnp.sum(
        expo_global, axis=-1, keepdims=True
    )
    probs_local = expo_local / totals
    probs_global = expo_global / totals
    weights_local = probs_local.astype(jnp.bfloat16)
    weights_global = probs_global.astype(jnp.bfloat16)
    attended = jnp.einsum(
        "bhqk,bkhd->bqhd", weights_local, local_vals, preferred_element_type=jnp.float32
    ) + jnp.einsum(
        "bhqk,khd->bqhd", weights_global, global_vals, preferred_element_type=jnp.float32
    )
    attn_out = attended.reshape(rows_dev, width_dev).astype(jnp.bfloat16)
    dprobs_local = jnp.einsum(
        "bqhd,bkhd->bhqk", grad_blocks, local_vals, preferred_element_type=jnp.float32
    )
    dprobs_global = jnp.einsum(
        "bqhd,khd->bhqk", grad_blocks, global_vals, preferred_element_type=jnp.float32
    )
    delta = jnp.sum(probs_local * dprobs_local, axis=-1, keepdims=True) + jnp.sum(
        probs_global * dprobs_global, axis=-1, keepdims=True
    )
    dscores_local = (probs_local * (dprobs_local - delta) * scale).astype(jnp.bfloat16)
    dscores_global = (probs_global * (dprobs_global - delta) * scale).astype(jnp.bfloat16)
    query_sum = jnp.einsum(
        "bhqk,bkhd->bqhd", dscores_local, local_keys, preferred_element_type=jnp.float32
    ) + jnp.einsum(
        "bhqk,khd->bqhd", dscores_global, global_keys, preferred_element_type=jnp.float32
    )
    query_grad = query_sum.reshape(rows_dev, width_dev).astype(jnp.bfloat16)
    local_dk = jnp.einsum(
        "bhqk,bqhd->bkhd", dscores_local, query_blocks, preferred_element_type=jnp.float32
    )
    local_dv = jnp.einsum(
        "bhqk,bqhd->bkhd", weights_local, grad_blocks, preferred_element_type=jnp.float32
    )
    local_grads = jnp.stack(
        [
            local_dk.reshape(blocks_dev, local_len, width_dev),
            local_dv.reshape(blocks_dev, local_len, width_dev),
        ],
        2,
    )
    before_terms = local_grads[:, :BLK].reshape(rows_dev, 2, width_dev)
    here_terms = local_grads[:, BLK : 2 * BLK].reshape(rows_dev, 2, width_dev)
    after_terms = local_grads[:, 2 * BLK : 3 * BLK].reshape(rows_dev, 2, width_dev)
    rims = jnp.concatenate([before_terms[:BLK], after_terms[rows_dev - BLK :]], 0)
    rim_padded = extended(rims.astype(jnp.bfloat16), (("seq", 0),), BLK).astype(rims.dtype)
    window_sum = (
        here_terms
        + jnp.concatenate([before_terms[BLK:], rim_padded[3 * BLK :]], 0)
        + jnp.concatenate([rim_padded[:BLK], after_terms[: rows_dev - BLK]], 0)
    )
    slot_grads = local_grads[:, 3 * BLK :].reshape(spots, BLK * 2 * width_dev).astype(jnp.bfloat16)
    placing = (
        my_places[:, None] == jnp.arange(seq_count * capacity, dtype=jnp.int32)[None, :]
    ).astype(jnp.bfloat16)
    to_send = jnp.einsum(
        "ts,tx->sx", placing, slot_grads, preferred_element_type=jnp.float32
    ).astype(jnp.bfloat16)
    returned = lax.all_to_all(
        to_send.reshape(seq_count, capacity, BLK * 2 * width_dev),
        "seq",
        split_axis=0,
        concat_axis=0,
        tiled=True,
    )
    landing = (
        incoming.reshape(-1)[:, None] == jnp.arange(blocks_dev, dtype=jnp.int32)[None, :]
    ).astype(jnp.bfloat16)
    random_sum = jnp.einsum(
        "sn,sx->nx",
        landing,
        returned.reshape(seq_count * capacity, BLK * 2 * width_dev),
        preferred_element_type=jnp.float32,
    ).reshape(rows_dev, 2, width_dev)
    global_dk = jnp.einsum(
        "bhqk,bqhd->khd", dscores_global, query_blocks, preferred_element_type=jnp.float32
    )
    global_dv = jnp.einsum(
        "bhqk,bqhd->khd", weights_global, grad_blocks, preferred_element_type=jnp.float32
    )
    global_terms = jnp.stack(
        [global_dk.reshape(global_len, width_dev), global_dv.reshape(global_len, width_dev)], 1
    )
    summed_all = lax.psum(global_terms, "seq")
    own_term = lax.dynamic_slice_in_dim(summed_all, my_index * GLEN, GLEN, 0)
    combined = window_sum + random_sum
    base_rows = lax.dynamic_slice_in_dim(combined, own_global * BLK, GLEN, 0)
    combined = lax.dynamic_update_slice_in_dim(combined, base_rows + own_term, own_global * BLK, 0)
    key_grad = combined[:, 0].astype(jnp.bfloat16)
    value_grad = combined[:, 1].astype(jnp.bfloat16)
    return (attn_out, query_grad, key_grad, value_grad)


def solution(mesh):
    in_specs = (
        P("seq", "head"),
        P("seq", "head"),
        P("seq", "head"),
        P("seq", "head"),
        P(),
        P("seq"),
    )
    out_specs = (P("seq", "head"), P("seq", "head"), P("seq", "head"), P("seq", "head"))
    return jax.shard_map(shards, mesh=mesh, in_specs=in_specs, out_specs=out_specs, check_vma=False)
```

profile of v0, /device:TPU:0, one launch (start us, length us, event | category | flops | bytes accessed | tf_op | source)
XLA Modules:
  0.0 270.9 jit_solution(358742052973094636)
XLA Ops:
  13.8 7.4 %all-to-all-start = ((bf16[8,2,64,2,512]{4,2,3,1,0:T(8,128)(2,1)}), bf16[8,2,64,2,512]{4,2,3,1,0:T(8,128)(2,1)S(1)}, u32[]{:S(2)}, u32[]{:S(2)}) async-start(bf16[8,2,64,2,512]{4,2,3,1,0:T(8,128)(2,1)} %broadcast_select_fusion), calls=%async_computation | async-start | bytes 4194304 | tf_op jit(solution)/shard_map/all_to_all | solution.py:62
  21.9 4.6 %collective-permute-start = (bf16[64,2,512]{2,0,1:T(8,128)(2,1)}, bf16[64,2,512]{2,0,1:T(8,128)(2,1)}, u32[]{:S(2)}, u32[]{:S(2)}) collective-permute-start(bf16[64,2,512]{2,0,1:T(8,128)(2,1)} %get-tuple-element.20), channel_id=1, source_target_pairs={{0,4},{4,8},{8,12},{12,16},{16,20},{20,24},{24,28},{1,5},{5,9},{9,... | collective-permute-start | bytes 393224 | tf_op jit(solution)/shard_map/ppermute | solution.py:19
  31.7 61.0 %all_gather.3 = bf16[128,2,512]{2,1,0:T(2,128)(2,1)S(1)} all-gather(bf16[16,2,512]{2,1,0:T(2,128)(2,1)S(1)} %copy.241), channel_id=1, replica_groups=mesh['seq'=8,'head'=4] {'seq'}, dimensions={0}, use_global_device_ids=true | all-gather | bytes 294912 | tf_op jit(solution)/shard_map/all_gather | solution.py:45
  111.8 2.4 fusion.20
  114.3 2.7 copy.237
  118.1 3.7 %fusion.1 = (f32[4,4,64]{2,1,0:T(4,128)}, f32[4,4,384,64]{2,3,1,0:T(8,128)}) fusion(f32[4,4,64]{2,1,0:T(4,128)S(1)} %copy_add_fusion.1, f32[4,4,64]{2,1,0:T(4,128)S(1)} %copy_maximum_fusion, f32[4,4,384,64]{2,3,1,0:T(8,128)S(1)} %get-tuple-element.29, bf16[4,384,4,128]{1,3,2,0:T(8,128)(2,1)} %bitcast.176, bf16[4,64,4,128]{3,2,1,0:T(4,128)(2,1)S(1)} %copy-done.17), kind=kOutput, calls=%fused_computation.15 | convolution fusion | flops 102235136 | bytes 4993024 | tf_op jit(solution)/shard_map/bqhd,bkhd->bhqk/dot_general | solution.py:112
  121.9 2.4 copy.267
  126.4 2.4 fusion.4
  128.8 2.3 fusion.28
  131.1 3.5 %copy.266 = f32[4,384,1,512]{3,1,2,0:T(8,128)} copy(f32[4,384,1,512]{1,3,0,2:T(8,128)} %bitcast.154) | data formatting | bytes 6291456 | tf_op jit(solution)/shard_map/stack;reshape | solution.py:135
  134.7 2.3 fusion
  138.6 2.8 %copy.272 = bf16[4,192,2,512]{3,2,1,0:T(2,128)(2,1)} copy(bf16[4,192,2,512]{3,1,2,0:T(8,128)(2,1)S(1)} %slice.123) | data formatting | bytes 3145728 | tf_op jit(solution)/shard_map/slice | solution.py:152
  141.5 5.7 %convert_element_type.59 = bf16[12,65536]{1,0:T(8,128)(2,1)} reshape(bf16[4,192,2,512]{3,2,1,0:T(2,128)(2,1)} %copy.272) | data formatting | bytes 3145728 | tf_op jit(solution)/shard_map/convert_element_type | solution.py:152
  147.2 3.8 %convolution_convert_fusion = bf16[16,65536]{1,0:T(8,128)(2,1)} fusion(bf16[12,65536]{1,0:T(8,128)(2,1)} %convert_element_type.59, s32[12]{0:T(128)} %get-tuple-element.24), kind=kOutput, calls=%fused_computation.2 | convolution fusion | flops 26214592 | bytes 3670064 | tf_op jit(solution)/shard_map/ts,tx->sx/dot_general | solution.py:156
  151.0 3.6 %reshape.224 = bf16[8,2,65536]{2,1,0:T(2,128)(2,1)} reshape(bf16[16,65536]{1,0:T(8,128)(2,1)} %convolution_convert_fusion) | data formatting | bytes 4194304 | tf_op jit(solution)/shard_map/reshape | solution.py:160
  154.6 4.4 %all-to-all-start.1 = ((bf16[8,2,65536]{2,1,0:T(2,128)(2,1)}), bf16[8,2,65536]{2,1,0:T(2,128)(2,1)}, u32[]{:S(2)}, u32[]{:S(2)}) async-start(bf16[8,2,65536]{2,1,0:T(2,128)(2,1)} %reshape.224), calls=%async_computation.1 | async-start | bytes 4194304 | tf_op jit(solution)/shard_map/all_to_all | solution.py:159
  168.0 2.9 %fusion.11 = bf16[4,64,4,128]{3,1,2,0:T(8,128)(2,1)S(1)} fusion(f32[4,64,4,128]{3,1,2,0:T(8,128)S(1)} %convolution_bitcast_fusion.2, bf16[4,384,4,128]{1,3,2,0:T(8,128)(2,1)} %bitcast.177, f32[4,4,384,64]{2,3,1,0:T(8,128)} %copy-done.2, f32[4,4,64]{2,1,0:T(4,128)S(1)} %copy_add_fusion.1, f32[4,4,64]{2,1,0:T(4,128)S(1)} %copy_maximum_fusion), kind=kOutput, calls=%fused_computation.33 | convolution fusion | flops 102105088 | bytes 3940352 | tf_op jit(solution)/shard_map/bhqk,bkhd->bqhd/dot_general | solution.py:106
  177.0 2.6 fusion.10
  182.7 3.8 %collective-permute-start.2 = (bf16[64,2,512]{2,0,1:T(8,128)(2,1)S(1)}, bf16[64,2,512]{2,0,1:T(8,128)(2,1)S(1)}, u32[]{:S(2)}, u32[]{:S(2)}) collective-permute-start(bf16[64,2,512]{2,0,1:T(8,128)(2,1)S(1)} %get-tuple-element.10), channel_id=1, source_target_pairs={{0,4},{4,8},{8,12},{12,16},{16,20},{20,24},{24,28},{1,5},{5,9},{9,... | collective-permute-start | bytes 393224 | tf_op jit(solution)/shard_map/ppermute | solution.py:19
  189.8 4.0 %collective-permute-done.3 = bf16[64,2,512]{2,0,1:T(8,128)(2,1)S(1)} collective-permute-done((bf16[64,2,512]{2,0,1:T(8,128)(2,1)S(1)}, bf16[64,2,512]{2,0,1:T(8,128)(2,1)S(1)}, u32[]{:S(2)}, u32[]{:S(2)}) %collective-permute-start.3) | collective-permute-done | bytes 131104 | tf_op jit(solution)/shard_map/ppermute | solution.py:20
  194.6 15.2 %all-to-all-done.1 = bf16[8,2,65536]{2,1,0:T(2,128)(2,1)} async-done(((bf16[8,2,65536]{2,1,0:T(2,128)(2,1)}), bf16[8,2,65536]{2,1,0:T(2,128)(2,1)}, u32[]{:S(2)}, u32[]{:S(2)}) %all-to-all-start.1) | async-done | bytes 2097184 | tf_op jit(solution)/shard_map/all_to_all | solution.py:159
  209.8 2.1 reshape.225
  213.4 2.4 reshape.226
  217.7 44.7 %all-reduce.2.cloned.1.call-done = f32[128,2,512]{2,0,1:T(8,128)} async-done(((f32[128,2,512]{2,0,1:T(8,128)}), f32[128,2,512]{2,0,1:T(8,128)}) %all-reduce.2.cloned.1.call-update) | async-done | bytes 524304 | tf_op jit(solution)/shard_map/psum | solution.py:184
  (151 shorter events, 63.3 us)
Async XLA Ops:
  13.8 7.4 %copy-start.8 = (bf16[256,512]{1,0:T(8,128)(2,1)S(1)}, bf16[256,512]{1,0:T(8,128)(2,1)}, u32[]{:S(2)}) copy-start(bf16[256,512]{1,0:T(8,128)(2,1)} %param.7) | copy-start | bytes 786436
  13.8 7.4 %copy-start.9 = (bf16[256,512]{1,0:T(8,128)(2,1)S(1)}, bf16[256,512]{1,0:T(8,128)(2,1)}, u32[]{:S(2)}) copy-start(bf16[256,512]{1,0:T(8,128)(2,1)} %param.8) | copy-start | bytes 786436
  13.8 88.7 %all-to-all-start = ((bf16[8,2,64,2,512]{4,2,3,1,0:T(8,128)(2,1)}), bf16[8,2,64,2,512]{4,2,3,1,0:T(8,128)(2,1)S(1)}, u32[]{:S(2)}, u32[]{:S(2)}) async-start(bf16[8,2,64,2,512]{4,2,3,1,0:T(8,128)(2,1)} %broadcast_select_fusion), calls=%async_computation | async-start | bytes 4194304 | tf_op jit(solution)/shard_map/all_to_all | solution.py:62
  21.1 8.9 %copy-start.20 = (bf16[256,512]{1,0:T(8,128)(2,1)S(1)}, bf16[256,512]{1,0:T(8,128)(2,1)}, u32[]{:S(2)}) copy-start(bf16[256,512]{1,0:T(8,128)(2,1)} %param.6) | copy-start | bytes 786436
  21.1 9.0 %copy-start.21 = (bf16[256,512]{1,0:T(8,128)(2,1)S(1)}, bf16[256,512]{1,0:T(8,128)(2,1)}, u32[]{:S(2)}) copy-start(bf16[256,512]{1,0:T(8,128)(2,1)} %param.9) | copy-start | bytes 786436
  21.9 78.6 %collective-permute-start = (bf16[64,2,512]{2,0,1:T(8,128)(2,1)}, bf16[64,2,512]{2,0,1:T(8,128)(2,1)}, u32[]{:S(2)}, u32[]{:S(2)}) collective-permute-start(bf16[64,2,512]{2,0,1:T(8,128)(2,1)} %get-tuple-element.20), channel_id=1, source_target_pairs={{0,4},{4,8},{8,12},{12,16},{16,20},{20,24},{24,28},{1,5},{5,9},{9,... | collective-permute-start | bytes 393224 | tf_op jit(solution)/shard_map/ppermute | solution.py:19
  26.5 74.1 %collective-permute-start.1 = (bf16[64,2,512]{2,0,1:T(8,128)(2,1)}, bf16[64,2,512]{2,0,1:T(8,128)(2,1)}, u32[]{:S(2)}, u32[]{:S(2)}) collective-permute-start(bf16[64,2,512]{2,0,1:T(8,128)(2,1)} %get-tuple-element.21), channel_id=1, source_target_pairs={{4,0},{8,4},{12,8},{16,12},{20,16},{24,20},{28,24},{5,1},{9,5},{13... | collective-permute-start | bytes 393224 | tf_op jit(solution)/shard_map/ppermute | solution.py:20
  30.2 65.9 %copy-start.15 = (bf16[4,64,4,128]{3,2,1,0:T(4,128)(2,1)}, bf16[4,64,4,128]{3,2,1,0:T(4,128)(2,1)S(1)}, u32[]{:S(2)}) copy-start(bf16[4,64,4,128]{3,2,1,0:T(4,128)(2,1)S(1)} %reshape.222) | copy-start | bytes 786436
  96.1 4.4 %copy-start.19 = (bf16[128,1,512]{0,2,1:T(8,128)(2,1)}, bf16[128,1,512]{0,2,1:T(8,128)(2,1)S(1)}, u32[]{:S(2)}) copy-start(bf16[128,1,512]{0,2,1:T(8,128)(2,1)S(1)} %copy.291) | copy-start | bytes 393220
  110.5 7.6 %copy-start.2 = (f32[4,4,384,64]{2,3,1,0:T(8,128)}, f32[4,4,384,64]{2,3,1,0:T(8,128)S(1)}, u32[]{:S(2)}) copy-start(f32[4,4,384,64]{2,3,1,0:T(8,128)S(1)} %get-tuple-element.29) | copy-start | bytes 4718596
  114.3 2.7 copy-start.5
  114.3 3.9 %copy-start.17 = (bf16[4,64,4,128]{3,2,1,0:T(4,128)(2,1)S(1)}, bf16[4,64,4,128]{3,2,1,0:T(4,128)(2,1)}, u32[]{:S(2)}) copy-start(bf16[4,64,4,128]{3,2,1,0:T(4,128)(2,1)} %copy-done.15) | copy-start | bytes 786436
  126.4 2.4 copy-start.22
  154.6 55.2 %all-to-all-start.1 = ((bf16[8,2,65536]{2,1,0:T(2,128)(2,1)}), bf16[8,2,65536]{2,1,0:T(2,128)(2,1)}, u32[]{:S(2)}, u32[]{:S(2)}) async-start(bf16[8,2,65536]{2,1,0:T(2,128)(2,1)} %reshape.224), calls=%async_computation.1 | async-start | bytes 4194304 | tf_op jit(solution)/shard_map/all_to_all | solution.py:159
  159.0 103.4 %all-reduce.2.cloned.1.call-start = ((), (), s32[]{:S(2)}) async-start(), calls=%async_computation.2 | async-start | bytes 1048576 | tf_op jit(solution)/shard_map/psum | solution.py:184
  168.0 3.9 %copy-start.10 = (f32[4,128,256]{1,2,0:S(1)}, f32[4,128,256]{1,2,0}, u32[]{:S(2)}) copy-start(f32[4,128,256]{1,2,0} %fusion.59) | copy-start | bytes 1572868
  168.0 3.9 %copy-start.11 = (f32[4,4,64,128]{3,2,0,1:T(8,128)S(1)}, f32[4,4,64,128]{3,2,0,1:T(8,128)}, u32[]{:S(2)}) copy-start(f32[4,4,64,128]{3,2,0,1:T(8,128)} %get-tuple-element.5) | copy-start | bytes 1572868
  168.0 3.9 %copy-start.23 = (f32[4,4,64]{2,0,1:T(4,128)S(1)}, f32[4,4,64]{2,0,1:T(4,128)}, u32[]{:S(2)}) copy-start(f32[4,4,64]{2,0,1:T(4,128)} %copy.260) | copy-start | bytes 12292
  173.0 3.7 %copy-start.14 = (bf16[4,4,64,128]{3,2,0,1:T(8,128)(2,1)S(1)}, bf16[4,4,64,128]{3,2,0,1:T(8,128)(2,1)}, u32[]{:S(2)}) copy-start(bf16[4,4,64,128]{3,2,0,1:T(8,128)(2,1)} %copy-done.13) | copy-start | bytes 786436
  177.0 3.5 %copy-start = (f32[4,384,1,512]{3,1,2,0:T(8,128)S(1)}, f32[4,384,1,512]{3,1,2,0:T(8,128)}, u32[]{:S(2)}) copy-start(f32[4,384,1,512]{3,1,2,0:T(8,128)} %copy.266) | copy-start | bytes 9437188
  182.7 7.1 %collective-permute-start.2 = (bf16[64,2,512]{2,0,1:T(8,128)(2,1)S(1)}, bf16[64,2,512]{2,0,1:T(8,128)(2,1)S(1)}, u32[]{:S(2)}, u32[]{:S(2)}) collective-permute-start(bf16[64,2,512]{2,0,1:T(8,128)(2,1)S(1)} %get-tuple-element.10), channel_id=1, source_target_pairs={{0,4},{4,8},{8,12},{12,16},{16,20},{20,24},{24,28},{1,5},{5,9},{9,... | collective-permute-start | bytes 393224 | tf_op jit(solution)/shard_map/ppermute | solution.py:19
  186.5 7.3 %collective-permute-start.3 = (bf16[64,2,512]{2,0,1:T(8,128)(2,1)S(1)}, bf16[64,2,512]{2,0,1:T(8,128)(2,1)S(1)}, u32[]{:S(2)}, u32[]{:S(2)}) collective-permute-start(bf16[64,2,512]{2,0,1:T(8,128)(2,1)S(1)} %get-tuple-element.11), channel_id=1, source_target_pairs={{4,0},{8,4},{12,8},{16,12},{20,16},{24,20},{28,24},{5,1},{9,5},{13... | collective-permute-start | bytes 393224 | tf_op jit(solution)/shard_map/ppermute | solution.py:20
  194.6 17.3 %copy-start.25 = (s32[16]{0:T(128)S(1)}, s32[16]{0:T(128)}, u32[]{:S(2)}) copy-start(s32[16]{0:T(128)} %sub.62) | copy-start | bytes 196
  213.4 2.4 copy-start.12
  (9 other events, 12.2 us)
Sparse Core Ops, SparseCore 0:
  176.9 85.3 all-reduce.1
where the time goes:
time: 272 us; the launch traced here: 271 us
  waiting for transfers between devices  63.9 us (23%)
  blocking collectives  61 us (22%)
  local copies, waits for them, and re-layouts  57.8 us (21%)
  matrix products  27.4 us (10%)
  other arithmetic  23 us (8%)
  starting transfers between devices  22.7 us (8%)
  between operations  15.2 us (6%)
    all_gather x1, blocking collectives, shards(): global_kv = lax.all_gather(mine, 'seq', axis=0, tiled=True)  61 us
    psum x1, waiting for transfers between devices, shards(): summed_all = lax.psum(global_terms, 'seq')  44.7 us
    all_to_all x1, waiting for transfers between devices, shards(): lax.all_to_all(to_send.reshape(seq_count, capacity, BLK * 2 * width_dev),...  15.2 us
    unnamed x57, local copies, waits for them, and re-layouts  8.55 us
    ppermute x2, starting transfers between devices, extended(): before = lax.ppermute(last, axis, up)  8.31 us
    all_to_all x1, starting transfers between devices, shards(): lax.all_to_all(outgoing, 'seq', split_axis=0, concat_axis=0, tiled=True)  7.38 us
    another operation x2, local copies, waits for them, and re-layouts, shards(): jnp.stack([local_dk.reshape(blocks_dev, local_len, width_dev), local_dv.r...  5.89 us
    convert_element_type x1, local copies, waits for them, and re-layouts, shards(): local_grads[:, 3 * BLK:].reshape(spots, BLK * 2 * width_dev)  5.73 us
  transfers between devices with their start and end apart: 7, of which 3 were waited for; matrix products, arithmetic and copies ran while one was open for 17% of the time, Pallas kernels for 0%

commit v1 on v0

--- a/solution.py
+++ b/solution.py
@@ -7,6 +7,22 @@
 HDIM = 128
 BLK = 64
 GLEN = 16
+
+
+def pairwise_exchange(value, axis, split, join):
+    ways, here = (lax.axis_size(axis), lax.axis_index(axis))
+    width = value.shape[split] // ways
+    dims = list(value.shape)
+    dims[split] = width
+    height = dims[join]
+    dims[join] = height * ways
+    full = jnp.zeros(dims, value.dtype)
+    for mask in range(ways):
+        part = lax.dynamic_slice_in_dim(value, (here ^ mask) * width, width, axis=split)
+        if mask:
+            part = lax.ppermute(part, axis, [(d, d ^ mask) for d in range(ways)])
+        full = lax.dynamic_update_slice_in_dim(full, part, (here ^ mask) * height, axis=join)
+    return full
 
 
 def extended(array, sides, width):
@@ -59,7 +75,7 @@
     incoming = jnp.sum(asked * (targets[:, :, None] + 1), axis=1) - 1
     block_kv = paired.reshape(blocks_dev, BLK, 2, width_dev)
     outgoing = jnp.take(block_kv, jnp.maximum(incoming, 0), axis=0)
-    received = lax.all_to_all(outgoing, "seq", split_axis=0, concat_axis=0, tiled=True)
+    received = pairwise_exchange(outgoing, "seq", 0, 0)
     fetched = jnp.take(received.reshape(seq_count * capacity, BLK, 2, width_dev), my_places, axis=0)
     fetched = fetched.reshape(blocks_dev, per_block * BLK, 2, width_dev)
     local_kv = jnp.concatenate([earlier, current, later, fetched], 1)

time: 272 us -> 275 us (1.011)
  blocking collectives: 61 us -> 31.6 us
  waiting for transfers between devices: 63.9 us -> 80.2 us
  starting transfers between devices: 22.7 us -> 29.8 us
  local copies, waits for them, and re-layouts: 57.8 us -> 64.7 us
    all_gather x1, blocking collectives: 61 us -> 31.6 us  [shards(): global_kv = lax.all_gather(mine, 'seq', axis=0, tiled=True)]
    ppermute x0 -> x7, waiting for transfers between devices: none -> 20 us  [pairwise_exchange(): part = lax.ppermute(part, axis, [(d, d ^ mask) for d in range(ways)])]
    ppermute x0 -> x7, starting transfers between devices: none -> 13.6 us  [pairwise_exchange(): part = lax.ppermute(part, axis, [(d, d ^ mask) for d in range(ways)])]
    all_to_all x1 -> x0, starting transfers between devices: 7.38 us -> none  [shards(): lax.all_to_all(outgoing, 'seq', split_axis=0, concat_axis=0, tiled=True)]
    psum x1, waiting for transfers between devices: 44.7 us -> 39.1 us  [shards(): summed_all = lax.psum(global_terms, 'seq')]
    dynamic_update_slice x0 -> x7, local copies, waits for them, and re-layouts: none -> 2.99 us  [pairwise_exchange(): lax.dynamic_update_slice_in_dim(full, part, (here ^ mask) * height, axis=...]
    unnamed x57 -> x67, local copies, waits for them, and re-layouts: 8.55 us -> 8.87 us
  transfers between devices with their start and end apart: 7 -> 13, of which waited for: 3 -> 7; matrix products, arithmetic and copies ran while one was open for 17% -> 21% of each run, Pallas kernels for 0% -> 0%
where the time goes in v1:
time: 275 us; the launch traced here: 273 us
  waiting for transfers between devices  80.2 us (29%)
  local copies, waits for them, and re-layouts  64.7 us (24%)
  blocking collectives  31.6 us (11%)
  starting transfers between devices  29.8 us (11%)
  matrix products  27.4 us (10%)
  other arithmetic  24.4 us (9%)
  between operations  15.4 us (6%)
    psum x1, waiting for transfers between devices, shards(): summed_all = lax.psum(global_terms, 'seq')  39.1 us
    all_gather x1, blocking collectives, shards(): global_kv = lax.all_gather(mine, 'seq', axis=0, tiled=True)  31.6 us
    ppermute x7, waiting for transfers between devices, pairwise_exchange(): part = lax.ppermute(part, axis, [(d, d ^ mask) for d in range(ways)])  20 us
    all_to_all x1, waiting for transfers between devices, shards(): lax.all_to_all(to_send.reshape(seq_count, capacity, BLK * 2 * width_dev),...  16.9 us
    ppermute x7, starting transfers between devices, pairwise_exchange(): part = lax.ppermute(part, axis, [(d, d ^ mask) for d in range(ways)])  13.6 us
    ppermute x2, starting transfers between devices, extended(): before = lax.ppermute(last, axis, up)  9.24 us
    unnamed x67, local copies, waits for them, and re-layouts  8.87 us
    another operation x2, local copies, waits for them, and re-layouts, shards(): jnp.stack([local_dk.reshape(blocks_dev, local_len, width_dev), local_dv.r...  5.88 us
  transfers between devices with their start and end apart: 13, of which 7 were waited for; matrix products, arithmetic and copies ran while one was open for 21% of the time, Pallas kernels for 0%

profile of v1, /device:TPU:0, one launch (start us, length us, event | category | flops | bytes accessed | tf_op | source)
XLA Modules:
  0.0 273.5 jit_solution(7377280141223135345)
XLA Ops:
  8.9 5.5 %collective-permute-start = (bf16[64,2,512]{2,0,1:T(8,128)(2,1)}, bf16[64,2,512]{2,0,1:T(8,128)(2,1)}, u32[]{:S(2)}, u32[]{:S(2)}) collective-permute-start(bf16[64,2,512]{2,0,1:T(8,128)(2,1)} %get-tuple-element.28), channel_id=1, source_target_pairs={{0,4},{4,8},{8,12},{12,16},{16,20},{20,24},{24,28},{1,5},{5,9},{9,... | collective-permute-start | bytes 393224 | tf_op jit(solution)/shard_map/ppermute | solution.py:35
  22.5 5.7 %collective-permute-start.8 = (bf16[1,2,64,2,512]{4,2,3,1,0:T(8,128)(2,1)}, bf16[1,2,64,2,512]{4,2,3,1,0:T(8,128)(2,1)}, u32[]{:S(2)}, u32[]{:S(2)}) collective-permute-start(bf16[1,2,64,2,512]{4,2,3,1,0:T(8,128)(2,1)} %get-tuple-element.14), channel_id=1, source_target_pairs={{0,28},{4,24},{8,20},{12,16},{16,12},{20,8},{24,4},{28,0},{1,29},{... | collective-permute-start | bytes 786440 | tf_op jit(solution)/shard_map/ppermute | solution.py:23
  32.7 31.6 %all_gather.3 = bf16[128,2,512]{2,1,0:T(2,128)(2,1)S(1)} all-gather(bf16[16,2,512]{2,1,0:T(2,128)(2,1)S(1)} %copy.241), channel_id=1, replica_groups=mesh['seq'=8,'head'=4] {'seq'}, dimensions={0}, use_global_device_ids=true | all-gather | bytes 294912 | tf_op jit(solution)/shard_map/all_gather | solution.py:61
  79.9 3.3 %collective-permute-start.5 = (bf16[1,2,64,2,512]{4,2,3,1,0:T(8,128)(2,1)}, bf16[1,2,64,2,512]{4,2,3,1,0:T(8,128)(2,1)S(1)}, u32[]{:S(2)}, u32[]{:S(2)}) collective-permute-start(bf16[1,2,64,2,512]{4,2,3,1,0:T(8,128)(2,1)} %get-tuple-element.17), channel_id=1, source_target_pairs={{0,16},{4,20},{8,24},{12,28},{16,0},{20,4},{24,8},{28,12},{1,17},{... | collective-permute-start | bytes 786440 | tf_op jit(solution)/shard_map/ppermute | solution.py:23
  89.2 14.8 %collective-permute-done.5 = bf16[1,2,64,2,512]{4,2,3,1,0:T(8,128)(2,1)S(1)} collective-permute-done((bf16[1,2,64,2,512]{4,2,3,1,0:T(8,128)(2,1)}, bf16[1,2,64,2,512]{4,2,3,1,0:T(8,128)(2,1)S(1)}, u32[]{:S(2)}, u32[]{:S(2)}) %collective-permute-start.5) | collective-permute-done | bytes 262176 | tf_op jit(solution)/shard_map/ppermute | solution.py:23
  104.0 3.0 %collective-permute-done.6 = bf16[1,2,64,2,512]{4,2,3,1,0:T(8,128)(2,1)S(1)} collective-permute-done((bf16[1,2,64,2,512]{4,2,3,1,0:T(8,128)(2,1)}, bf16[1,2,64,2,512]{4,2,3,1,0:T(8,128)(2,1)S(1)}, u32[]{:S(2)}, u32[]{:S(2)}) %collective-permute-start.6) | collective-permute-done | bytes 262176 | tf_op jit(solution)/shard_map/ppermute | solution.py:23
  117.8 2.4 fusion.20
  120.2 2.7 copy.237
  124.1 3.8 %fusion.1 = (f32[4,4,64]{2,1,0:T(4,128)}, f32[4,4,384,64]{2,3,1,0:T(8,128)}) fusion(f32[4,4,64]{2,1,0:T(4,128)S(1)} %copy_add_fusion.1, f32[4,4,64]{2,1,0:T(4,128)S(1)} %copy_maximum_fusion, f32[4,4,384,64]{2,3,1,0:T(8,128)S(1)} %get-tuple-element.37, bf16[4,384,4,128]{1,3,2,0:T(8,128)(2,1)} %bitcast.176, bf16[4,64,4,128]{3,2,1,0:T(4,128)(2,1)S(1)} %copy-done.17), kind=kOutput, calls=%fused_computation.15 | convolution fusion | flops 102235136 | bytes 4993024 | tf_op jit(solution)/shard_map/bqhd,bkhd->bhqk/dot_general | solution.py:128
  127.9 2.4 copy.267
  132.4 2.4 fusion.4
  134.8 2.3 fusion.28
  137.1 3.5 %copy.266 = f32[4,384,1,512]{3,1,2,0:T(8,128)} copy(f32[4,384,1,512]{1,3,0,2:T(8,128)} %bitcast.154) | data formatting | bytes 6291456 | tf_op jit(solution)/shard_map/stack;reshape | solution.py:151
  144.7 2.8 %copy.272 = bf16[4,192,2,512]{3,2,1,0:T(2,128)(2,1)} copy(bf16[4,192,2,512]{3,1,2,0:T(8,128)(2,1)S(1)} %slice.123) | data formatting | bytes 3145728 | tf_op jit(solution)/shard_map/slice | solution.py:168
  147.6 5.8 %convert_element_type.59 = bf16[12,65536]{1,0:T(8,128)(2,1)} reshape(bf16[4,192,2,512]{3,2,1,0:T(2,128)(2,1)} %copy.272) | data formatting | bytes 3145728 | tf_op jit(solution)/shard_map/convert_element_type | solution.py:168
  153.3 3.8 %convolution_convert_fusion = bf16[16,65536]{1,0:T(8,128)(2,1)} fusion(bf16[12,65536]{1,0:T(8,128)(2,1)} %convert_element_type.59, s32[12]{0:T(128)} %get-tuple-element.32), kind=kOutput, calls=%fused_computation.2 | convolution fusion | flops 26214592 | bytes 3670064 | tf_op jit(solution)/shard_map/ts,tx->sx/dot_general | solution.py:172
  157.1 3.6 %reshape.224 = bf16[8,2,65536]{2,1,0:T(2,128)(2,1)} reshape(bf16[16,65536]{1,0:T(8,128)(2,1)} %convolution_convert_fusion) | data formatting | bytes 4194304 | tf_op jit(solution)/shard_map/reshape | solution.py:176
  160.8 4.4 %all-to-all-start = ((bf16[8,2,65536]{2,1,0:T(2,128)(2,1)}), bf16[8,2,65536]{2,1,0:T(2,128)(2,1)}, u32[]{:S(2)}, u32[]{:S(2)}) async-start(bf16[8,2,65536]{2,1,0:T(2,128)(2,1)} %reshape.224), calls=%async_computation | async-start | bytes 4194304 | tf_op jit(solution)/shard_map/all_to_all | solution.py:175
  174.2 2.9 %fusion.11 = bf16[4,64,4,128]{3,1,2,0:T(8,128)(2,1)S(1)} fusion(f32[4,64,4,128]{3,1,2,0:T(8,128)S(1)} %convolution_bitcast_fusion.2, bf16[4,384,4,128]{1,3,2,0:T(8,128)(2,1)} %bitcast.177, f32[4,4,384,64]{2,3,1,0:T(8,128)} %copy-done.2, f32[4,4,64]{2,1,0:T(4,128)S(1)} %copy_add_fusion.1, f32[4,4,64]{2,1,0:T(4,128)S(1)} %copy_maximum_fusion), kind=kOutput, calls=%fused_computation.33 | convolution fusion | flops 102105088 | bytes 3940352 | tf_op jit(solution)/shard_map/bhqk,bkhd->bqhd/dot_general | solution.py:122
  183.2 2.6 fusion.10
  188.9 3.8 %collective-permute-start.9 = (bf16[64,2,512]{2,0,1:T(8,128)(2,1)S(1)}, bf16[64,2,512]{2,0,1:T(8,128)(2,1)S(1)}, u32[]{:S(2)}, u32[]{:S(2)}) collective-permute-start(bf16[64,2,512]{2,0,1:T(8,128)(2,1)S(1)} %get-tuple-element.10), channel_id=1, source_target_pairs={{0,4},{4,8},{8,12},{12,16},{16,20},{20,24},{24,28},{1,5},{5,9},{9,... | collective-permute-start | bytes 393224 | tf_op jit(solution)/shard_map/ppermute | solution.py:35
  196.3 3.9 %collective-permute-done.10 = bf16[64,2,512]{2,0,1:T(8,128)(2,1)S(1)} collective-permute-done((bf16[64,2,512]{2,0,1:T(8,128)(2,1)S(1)}, bf16[64,2,512]{2,0,1:T(8,128)(2,1)S(1)}, u32[]{:S(2)}, u32[]{:S(2)}) %collective-permute-start.10) | collective-permute-done | bytes 131104 | tf_op jit(solution)/shard_map/ppermute | solution.py:36
  201.0 16.9 %all-to-all-done = bf16[8,2,65536]{2,1,0:T(2,128)(2,1)} async-done(((bf16[8,2,65536]{2,1,0:T(2,128)(2,1)}), bf16[8,2,65536]{2,1,0:T(2,128)(2,1)}, u32[]{:S(2)}, u32[]{:S(2)}) %all-to-all-start) | async-done | bytes 2097184 | tf_op jit(solution)/shard_map/all_to_all | solution.py:175
  225.8 39.1 %all-reduce.2.cloned.1.call-done = f32[128,2,512]{2,0,1:T(8,128)} async-done(((f32[128,2,512]{2,0,1:T(8,128)}), f32[128,2,512]{2,0,1:T(8,128)}) %all-reduce.2.cloned.1.call-update) | async-done | bytes 524304 | tf_op jit(solution)/shard_map/psum | solution.py:200
  (182 shorter events, 85.4 us)
Async XLA Ops:
  8.9 67.2 %collective-permute-start = (bf16[64,2,512]{2,0,1:T(8,128)(2,1)}, bf16[64,2,512]{2,0,1:T(8,128)(2,1)}, u32[]{:S(2)}, u32[]{:S(2)}) collective-permute-start(bf16[64,2,512]{2,0,1:T(8,128)(2,1)} %get-tuple-element.28), channel_id=1, source_target_pairs={{0,4},{4,8},{8,12},{12,16},{16,20},{20,24},{24,28},{1,5},{5,9},{9,... | collective-permute-start | bytes 393224 | tf_op jit(solution)/shard_map/ppermute | solution.py:35
  14.3 62.3 %collective-permute-start.1 = (bf16[64,2,512]{2,0,1:T(8,128)(2,1)}, bf16[64,2,512]{2,0,1:T(8,128)(2,1)}, u32[]{:S(2)}, u32[]{:S(2)}) collective-permute-start(bf16[64,2,512]{2,0,1:T(8,128)(2,1)} %get-tuple-element.29), channel_id=1, source_target_pairs={{4,0},{8,4},{12,8},{16,12},{20,16},{24,20},{28,24},{5,1},{9,5},{13... | collective-permute-start | bytes 393224 | tf_op jit(solution)/shard_map/ppermute | solution.py:36
  21.2 11.4 %copy-start.8 = (bf16[256,512]{1,0:T(8,128)(2,1)S(1)}, bf16[256,512]{1,0:T(8,128)(2,1)}, u32[]{:S(2)}) copy-start(bf16[256,512]{1,0:T(8,128)(2,1)} %param.7) | copy-start | bytes 786436
  21.2 11.4 %copy-start.9 = (bf16[256,512]{1,0:T(8,128)(2,1)S(1)}, bf16[256,512]{1,0:T(8,128)(2,1)}, u32[]{:S(2)}) copy-start(bf16[256,512]{1,0:T(8,128)(2,1)} %param.8) | copy-start | bytes 786436
  21.2 43.0 %copy-start.20 = (bf16[256,512]{1,0:T(8,128)(2,1)S(1)}, bf16[256,512]{1,0:T(8,128)(2,1)}, u32[]{:S(2)}) copy-start(bf16[256,512]{1,0:T(8,128)(2,1)} %param.6) | copy-start | bytes 786436
  22.5 84.5 %collective-permute-start.8 = (bf16[1,2,64,2,512]{4,2,3,1,0:T(8,128)(2,1)}, bf16[1,2,64,2,512]{4,2,3,1,0:T(8,128)(2,1)}, u32[]{:S(2)}, u32[]{:S(2)}) collective-permute-start(bf16[1,2,64,2,512]{4,2,3,1,0:T(8,128)(2,1)} %get-tuple-element.14), channel_id=1, source_target_pairs={{0,28},{4,24},{8,20},{12,16},{16,12},{20,8},{24,4},{28,0},{1,29},{... | collective-permute-start | bytes 786440 | tf_op jit(solution)/shard_map/ppermute | solution.py:23
  28.2 55.9 %collective-permute-start.3 = (bf16[1,2,64,2,512]{4,2,3,1,0:T(8,128)(2,1)}, bf16[1,2,64,2,512]{4,2,3,1,0:T(8,128)(2,1)}, u32[]{:S(2)}, u32[]{:S(2)}) collective-permute-start(bf16[1,2,64,2,512]{4,2,3,1,0:T(8,128)(2,1)} %get-tuple-element.19), channel_id=1, source_target_pairs={{0,8},{4,12},{8,0},{12,4},{16,24},{20,28},{24,16},{28,20},{1,9},{5... | collective-permute-start | bytes 786440 | tf_op jit(solution)/shard_map/ppermute | solution.py:23
  28.2 51.7 %collective-permute-start.2 = (bf16[1,2,64,2,512]{4,2,3,1,0:T(8,128)(2,1)}, bf16[1,2,64,2,512]{4,2,3,1,0:T(8,128)(2,1)}, u32[]{:S(2)}, u32[]{:S(2)}) collective-permute-start(bf16[1,2,64,2,512]{4,2,3,1,0:T(8,128)(2,1)} %get-tuple-element.20), channel_id=1, source_target_pairs={{0,4},{4,0},{8,12},{12,8},{16,20},{20,16},{24,28},{28,24},{1,5},{5... | collective-permute-start | bytes 786440 | tf_op jit(solution)/shard_map/ppermute | solution.py:23
  65.4 7.2 %copy-start.15 = (bf16[4,64,4,128]{3,2,1,0:T(4,128)(2,1)}, bf16[4,64,4,128]{3,2,1,0:T(4,128)(2,1)S(1)}, u32[]{:S(2)}) copy-start(bf16[4,64,4,128]{3,2,1,0:T(4,128)(2,1)S(1)} %reshape.222) | copy-start | bytes 786436
  68.1 6.5 %copy-start.30 = (pred[4]{0:T(512)(128)(4,1)S(1)}, pred[4]{0:T(512)(128)(4,1)}, u32[]{:S(2)}) copy-start(pred[4]{0:T(512)(128)(4,1)} %get-tuple-element.40) | copy-start | bytes 16
  68.1 6.6 %copy-start.28 = (pred[384]{0:T(512)(128)(4,1)S(1)}, pred[384]{0:T(512)(128)(4,1)}, u32[]{:S(2)}) copy-start(pred[384]{0:T(512)(128)(4,1)} %pad.15.clone) | copy-start | bytes 1156
  68.1 6.6 %copy-start.29 = (pred[384]{0:T(512)(128)(4,1)S(1)}, pred[384]{0:T(512)(128)(4,1)}, u32[]{:S(2)}) copy-start(pred[384]{0:T(512)(128)(4,1)} %pad.13.clone) | copy-start | bytes 1156
  68.1 7.2 %copy-start.26 = (pred[4,3]{1,0:T(4,128)(4,1)S(1)}, pred[4,3]{1,0:T(4,128)(4,1)}, u32[]{:S(2)}) copy-start(pred[4,3]{1,0:T(4,128)(4,1)} %compare_and_fusion) | copy-start | bytes 40
  70.3 6.3 %copy-start.19 = (bf16[128,1,512]{0,2,1:T(8,128)(2,1)}, bf16[128,1,512]{0,2,1:T(8,128)(2,1)S(1)}, u32[]{:S(2)}) copy-start(bf16[128,1,512]{0,2,1:T(8,128)(2,1)S(1)} %copy.291) | copy-start | bytes 393220
  76.1 31.0 %collective-permute-start.7 = (bf16[1,2,64,2,512]{4,2,3,1,0:T(8,128)(2,1)}, bf16[1,2,64,2,512]{4,2,3,1,0:T(8,128)(2,1)S(1)}, u32[]{:S(2)}, u32[]{:S(2)}) collective-permute-start(bf16[1,2,64,2,512]{4,2,3,1,0:T(8,128)(2,1)} %get-tuple-element.15), channel_id=1, source_target_pairs={{0,24},{4,28},{8,16},{12,20},{16,8},{20,12},{24,0},{28,4},{1,25},{... | collective-permute-start | bytes 786440 | tf_op jit(solution)/shard_map/ppermute | solution.py:23
  76.6 12.5 %collective-permute-start.4 = (bf16[1,2,64,2,512]{4,2,3,1,0:T(8,128)(2,1)}, bf16[1,2,64,2,512]{4,2,3,1,0:T(8,128)(2,1)S(1)}, u32[]{:S(2)}, u32[]{:S(2)}) collective-permute-start(bf16[1,2,64,2,512]{4,2,3,1,0:T(8,128)(2,1)} %get-tuple-element.18), channel_id=1, source_target_pairs={{0,12},{4,8},{8,4},{12,0},{16,28},{20,24},{24,20},{28,16},{1,13},{... | collective-permute-start | bytes 786440 | tf_op jit(solution)/shard_map/ppermute | solution.py:23
  79.9 24.1 %collective-permute-start.5 = (bf16[1,2,64,2,512]{4,2,3,1,0:T(8,128)(2,1)}, bf16[1,2,64,2,512]{4,2,3,1,0:T(8,128)(2,1)S(1)}, u32[]{:S(2)}, u32[]{:S(2)}) collective-permute-start(bf16[1,2,64,2,512]{4,2,3,1,0:T(8,128)(2,1)} %get-tuple-element.17), channel_id=1, source_target_pairs={{0,16},{4,20},{8,24},{12,28},{16,0},{20,4},{24,8},{28,12},{1,17},{... | collective-permute-start | bytes 786440 | tf_op jit(solution)/shard_map/ppermute | solution.py:23
  84.1 22.9 %collective-permute-start.6 = (bf16[1,2,64,2,512]{4,2,3,1,0:T(8,128)(2,1)}, bf16[1,2,64,2,512]{4,2,3,1,0:T(8,128)(2,1)S(1)}, u32[]{:S(2)}, u32[]{:S(2)}) collective-permute-start(bf16[1,2,64,2,512]{4,2,3,1,0:T(8,128)(2,1)} %get-tuple-element.16), channel_id=1, source_target_pairs={{0,20},{4,16},{8,28},{12,24},{16,4},{20,0},{24,12},{28,8},{1,21},{... | collective-permute-start | bytes 786440 | tf_op jit(solution)/shard_map/ppermute | solution.py:23
  115.8 8.4 %copy-start.2 = (f32[4,4,384,64]{2,3,1,0:T(8,128)}, f32[4,4,384,64]{2,3,1,0:T(8,128)S(1)}, u32[]{:S(2)}) copy-start(f32[4,4,384,64]{2,3,1,0:T(8,128)S(1)} %get-tuple-element.37) | copy-start | bytes 4718596
  160.8 57.2 %all-to-all-start = ((bf16[8,2,65536]{2,1,0:T(2,128)(2,1)}), bf16[8,2,65536]{2,1,0:T(2,128)(2,1)}, u32[]{:S(2)}, u32[]{:S(2)}) async-start(bf16[8,2,65536]{2,1,0:T(2,128)(2,1)} %reshape.224), calls=%async_computation | async-start | bytes 4194304 | tf_op jit(solution)/shard_map/all_to_all | solution.py:175
  165.1 99.7 %all-reduce.2.cloned.1.call-start = ((), (), s32[]{:S(2)}) async-start(), calls=%async_computation.1 | async-start | bytes 1048576 | tf_op jit(solution)/shard_map/psum | solution.py:200
  188.9 7.4 %collective-permute-start.9 = (bf16[64,2,512]{2,0,1:T(8,128)(2,1)S(1)}, bf16[64,2,512]{2,0,1:T(8,128)(2,1)S(1)}, u32[]{:S(2)}, u32[]{:S(2)}) collective-permute-start(bf16[64,2,512]{2,0,1:T(8,128)(2,1)S(1)} %get-tuple-element.10), channel_id=1, source_target_pairs={{0,4},{4,8},{8,12},{12,16},{16,20},{20,24},{24,28},{1,5},{5,9},{9,... | collective-permute-start | bytes 393224 | tf_op jit(solution)/shard_map/ppermute | solution.py:35
  192.7 7.6 %collective-permute-start.10 = (bf16[64,2,512]{2,0,1:T(8,128)(2,1)S(1)}, bf16[64,2,512]{2,0,1:T(8,128)(2,1)S(1)}, u32[]{:S(2)}, u32[]{:S(2)}) collective-permute-start(bf16[64,2,512]{2,0,1:T(8,128)(2,1)S(1)} %get-tuple-element.11), channel_id=1, source_target_pairs={{4,0},{8,4},{12,8},{16,12},{20,16},{24,20},{28,24},{5,1},{9,5},{13... | collective-permute-start | bytes 393224 | tf_op jit(solution)/shard_map/ppermute | solution.py:36
  201.0 19.0 %copy-start.27 = (s32[16]{0:T(128)S(1)}, s32[16]{0:T(128)}, u32[]{:S(2)}) copy-start(s32[16]{0:T(128)} %sub.62) | copy-start | bytes 196
  (20 other events, 52.3 us)
Sparse Core Ops, SparseCore 0:
  183.1 81.7 all-reduce.1
